TPU v7x, 32 devices: a whole 2x2x4 slice. The times are simulated.
32 devices in a mesh: seq: 8 (over y, x, core), mp: 4 (over z).
Axes of the slice: x: 2, y: 2, z: 4, core: 2. Of those that a mesh axis runs over, the one named last changes fastest.
Arguments:
- qkv: bfloat16 [3, 8192, 8192], P(None, 'mp', 'seq'), may hold values from -6 to 6
- short_taps: bfloat16 [3, 8192, 7], P(None, 'mp'), may hold values from -2 to 2
- medium_taps: bfloat16 [8192, 128], P('mp'), may hold values from -0.5 to 0.5
- skip_gain: float32 [8192], P('mp'), may hold values from -4 to 4
- w_out: bfloat16 [8192, 8192], P('mp'), may hold values from -0.09375 to 0.09375
- resid: bfloat16 [8192, 8192], P('mp', 'seq'), may hold values from -6 to 6
- steer: float32 [8192], P('mp'), may hold values from -5 to 5
Outputs:
- layer_out: bfloat16 [8192, 8192], P('mp', 'seq')
All inputs are finite; a program needn't handle non-finite values.
Results may differ from a plain program's by a relative error of at most 0.017.
Values may be sent and summed in bfloat16 or wider, within the bound.
A program may use at most 192 MiB of HBM per device.

v0:
```python
import functools

import jax
import jax.numpy as jnp
from jax import lax
from jax.experimental import pallas as pl
from jax.experimental.pallas import tpu as pltpu
from jax.sharding import PartitionSpec as P

STAPS = 7
MTAPS = 128
LANES = 128
F32 = jnp.float32
BF16 = jnp.bfloat16


def from_behind(value, axis, steps):
    count = lax.axis_size(axis)
    return lax.ppermute(value, axis, [(source, source + steps) for source in range(count - steps)])


def chunks(slab):
    sizes = [1]
    left = slab // LANES - 3
    while left > 0:
        sizes.append(min(left, 2 if len(sizes) == 1 else 3))
        left -= sizes[-1]
    sizes.append(2)
    plan, end = [], slab
    for size in sizes:
        end -= size * LANES
        plan.append((end, size * LANES))
    return plan


def feature_kernel(blocks, *refs):
    token_refs = refs[:blocks]
    short_ref, medium_ref, y_ref, wide, kv = refs[blocks:]
    for at, ref in enumerate(token_refs):
        for s in range(3):
            if s > 0 or at > 0:
                wide[s, at * LANES : (at + 1) * LANES] = ref[s].astype(F32).T

    def short(s, row):
        total = short_ref[s, 0:1] * wide[s, row : row + LANES]
        for j in range(1, STAPS):
            total = total + short_ref[s, j : j + 1] * wide[s, row - j : row - j + LANES]
        return total

    for at in range(1, blocks):
        row = at * LANES
        kv[row - LANES : row] = (short(1, row) * short(2, row)).astype(BF16).astype(F32)

    for at in range(blocks - 2):
        row = at * LANES
        total = jnp.zeros((LANES, LANES), F32)
        for low in range(8):
            start = row + 8 - low
            block = kv[start : start + LANES + MTAPS - 8]
            for high in range(0, MTAPS, 8):
                first = MTAPS - 8 - high
                total = total + medium_ref[high + low : high + low + 1] * block[first : first + LANES]
        y_ref[row : row + LANES] = (short(0, row + 2 * LANES) * total).astype(BF16)


def features(sources, short, medium):
    channels = short.shape[2]
    blocks = len(sources)
    tokens = (blocks - 2) * LANES
    return pl.pallas_call(
        functools.partial(feature_kernel, blocks),
        grid=(channels // LANES,),
        in_specs=[pl.BlockSpec((3, LANES, LANES), lambda c, at=at: (0, c, at)) for _, at in sources]
        + [
            pl.BlockSpec((3, STAPS, LANES), lambda c: (0, 0, c)),
            pl.BlockSpec((MTAPS, LANES), lambda c: (0, c)),
        ],
        out_specs=pl.BlockSpec((tokens, LANES), lambda c: (0, c)),
        out_shape=jax.ShapeDtypeStruct((tokens, channels), BF16),
        scratch_shapes=[
            pltpu.VMEM((3, blocks * LANES, LANES), F32),
            pltpu.VMEM(((blocks - 1) * LANES, LANES), F32),
        ],
        cost_estimate=pl.CostEstimate(
            flops=2 * channels * tokens * (MTAPS + 4 * STAPS),
            bytes_accessed=6 * channels * blocks * LANES,
            transcendentals=0,
        ),
    )(*[array for array, _ in sources], short, medium)


def finish_kernel(*refs):
    resid_ref, steer_ref, proj_ref, out_ref = refs[0], refs[1], refs[2], refs[-1]
    gain = proj_ref[...].astype(F32) + steer_ref[...]
    out_ref[...] = (resid_ref[...].astype(F32) + gain.T).astype(BF16)


def finish(resid, steer, proj, out, first):
    tokens, channels = proj.shape
    rows = min(channels, 1024)
    at = first // LANES
    column = pl.BlockSpec((rows, LANES), lambda t, c: (c, at + t))
    specs = [
        column,
        pl.BlockSpec((1, rows), lambda t, c: (0, c)),
        pl.BlockSpec((LANES, rows), lambda t, c: (t, c)),
    ]
    held = [] if out is None else [out]
    return pl.pallas_call(
        finish_kernel,
        grid=(tokens // LANES, channels // rows),
        in_specs=specs + [pl.BlockSpec(memory_space=pl.ANY)] * len(held),
        out_specs=column,
        out_shape=jax.ShapeDtypeStruct(resid.shape, BF16),
        input_output_aliases={3: 0} if held else {},
        cost_estimate=pl.CostEstimate(
            flops=2 * channels * tokens, bytes_accessed=6 * channels * tokens, transcendentals=0
        ),
    )(resid, steer, proj, *held)


def shards(qkv, short_taps, medium_taps, skip_gain, w_out, resid, steer):
    slab = qkv.shape[2]
    short = jnp.swapaxes(short_taps.astype(F32), 1, 2)
    medium = medium_taps.astype(F32)
    medium = jnp.concatenate([medium[:, :1] + skip_gain[:, None], medium[:, 1:]], 1).T
    rim = from_behind(qkv[:, :, slab - 2 * LANES :], "seq", 1)
    out = None
    projs = []
    for first, tokens in chunks(slab):
        at = first // LANES
        sources = [(rim, i + 2) if i < 0 else (qkv, i) for i in range(at - 2, at + tokens // LANES)]
        y = features(sources, short, medium)
        part = jnp.dot(y, w_out, preferred_element_type=F32).astype(BF16)
        proj = lax.psum_scatter(part, "mp", scatter_dimension=1, tiled=True)
        projs.append((first, proj))
    for first, proj in projs:
        out = finish(resid, steer[None], proj, out, first)
    return out


def solution(mesh):
    return jax.shard_map(
        shards,
        mesh=mesh,
        in_specs=(
            P(None, "mp", "seq"),
            P(None, "mp", None),
            P("mp", None),
            P("mp"),
            P("mp", None),
            P("mp", "seq"),
            P("mp"),
        ),
        out_specs=P("mp", "seq"),
        check_vma=False,
    )
```

profile of v0, /device:TPU:9, one launch (start us, length us, event | category | flops | bytes accessed | tf_op | source)
XLA Modules:
  0.0 380.4 jit_solution(6992846496144260121)
XLA Ops:
  6.5 1.2 copy.11
  7.8 0.1 slice.13
  7.9 0.1 convert_element_type.16
  8.0 1.6 convert_bitcast_fusion.refs_4_.refs_5_.refs_3_
  9.6 0.7 slice_add_fusion
  10.3 1.1 maximum_bitcast_fusion.refs_5_.refs_6_.refs_4_
  11.4 18.4 %shard_map.76 = bf16[128,2048]{1,0:T(8,128)(2,1)} custom-call(bf16[3,2048,1024]{2,1,0:T(8,128)(2,1)} %refs_2_.7, bf16[3,2048,1024]{2,1,0:T(8,128)(2,1)} %refs_2_.7, bf16[3,2048,1024]{2,1,0:T(8,128)(2,1)} %refs_2_.7, f32[3,7,2048]{2,1,0:T(8,128)} %convert_bitcast_fusion.refs_4_.refs_5_.refs_3_, f32[128,2048]{1,0:T(8,128)} %maximum_bitcast_fusion.refs_5_.refs_6_.refs_4_), custom_call_target="tpu_custom_call" | custom-call | flops 81788928 | bytes 4718592 | tf_op jit(solution)/shard_map/pallas_call | solution.py:70
  29.8 16.6 %convolution_convert_fusion.3 = bf16[128,8192]{1,0:T(8,128)(2,1)} fusion(bf16[128,2048]{1,0:T(8,128)(2,1)} %shard_map.76, bf16[2048,8192]{1,0:T(8,128)(2,1)} %param.11), kind=kOutput, calls=%fused_computation.3 | convolution fusion | flops 4296015872 | bytes 36175872 | tf_op jit(solution)/shard_map/dot_general | solution.py:134
  46.4 0.0 reduce-scatter.11.cloned.1.call-update
  46.4 0.2 reduce-scatter.9.cloned.1.call-start
  46.6 35.1 %shard_map.75 = bf16[256,2048]{1,0:T(8,128)(2,1)} custom-call(bf16[3,2048,1024]{2,1,0:T(8,128)(2,1)} %refs_2_.7, bf16[3,2048,1024]{2,1,0:T(8,128)(2,1)} %refs_2_.7, bf16[3,2048,1024]{2,1,0:T(8,128)(2,1)} %refs_2_.7, bf16[3,2048,1024]{2,1,0:T(8,128)(2,1)} %refs_2_.7, f32[3,7,2048]{2,1,0:T(8,128)} %convert_bitcast_fusion.refs_4_.refs_5_.refs_3_, ...), custom_call_target="tpu_custom_call" | custom-call | flops 163577856 | bytes 6291456 | tf_op jit(solution)/shard_map/pallas_call | solution.py:70
  81.8 16.9 %convolution_convert_fusion.1 = bf16[256,8192]{1,0:T(8,128)(2,1)} fusion(bf16[256,2048]{1,0:T(8,128)(2,1)} %shard_map.75, bf16[2048,8192]{1,0:T(8,128)(2,1)} %param.11), kind=kOutput, calls=%fused_computation.1 | convolution fusion | flops 8592031744 | bytes 38797312 | tf_op jit(solution)/shard_map/dot_general | solution.py:134
  98.6 0.0 reduce-scatter.9.cloned.1.call-update
  98.6 0.3 reduce-scatter.7.cloned.1.call-start
  98.9 46.9 %shard_map.74 = bf16[384,2048]{1,0:T(8,128)(2,1)} custom-call(bf16[3,2048,1024]{2,1,0:T(8,128)(2,1)} %refs_2_.7, bf16[3,2048,1024]{2,1,0:T(8,128)(2,1)} %refs_2_.7, bf16[3,2048,1024]{2,1,0:T(8,128)(2,1)} %refs_2_.7, bf16[3,2048,1024]{2,1,0:T(8,128)(2,1)} %refs_2_.7, bf16[3,2048,1024]{2,1,0:T(8,128)(2,1)} %refs_2_.7, ...), custom_call_target="tpu_custom_call" | custom-call | flops 245366784 | bytes 7864320 | tf_op jit(solution)/shard_map/pallas_call | solution.py:70
  145.8 21.3 %convolution_convert_fusion = bf16[384,8192]{1,0:T(8,128)(2,1)} fusion(bf16[384,2048]{1,0:T(8,128)(2,1)} %shard_map.74, bf16[2048,8192]{1,0:T(8,128)(2,1)} %param.11), kind=kOutput, calls=%fused_computation | convolution fusion | flops 12888047616 | bytes 41418752 | tf_op jit(solution)/shard_map/dot_general | solution.py:134
  167.1 0.0 reduce-scatter.7.cloned.1.call-update
  167.1 0.0 reduce-scatter.5.cloned.1.call-start
  167.1 2.1 slice.9
  169.2 3.9 %collective-permute-start = (bf16[3,2048,256]{2,1,0:T(8,128)(2,1)S(1)}, bf16[3,2048,256]{2,1,0:T(8,128)(2,1)S(1)}, u32[]{:S(2)}, u32[]{:S(2)}) collective-permute-start(bf16[3,2048,256]{2,1,0:T(8,128)(2,1)S(1)} %slice.9), channel_id=1, source_target_pairs={{0,4},{4,8},{8,12},{12,16},{16,20},{20,24},{24,28},{1,5},{5,9},{9,... | collective-permute-start | bytes 9437192 | tf_op jit(solution)/shard_map/ppermute | solution.py:19
  173.2 33.9 %collective-permute-done.refs_0_.refs_1_ = bf16[3,2048,256]{2,1,0:T(8,128)(2,1)S(1)} collective-permute-done((bf16[3,2048,256]{2,1,0:T(8,128)(2,1)S(1)}, bf16[3,2048,256]{2,1,0:T(8,128)(2,1)S(1)}, u32[]{:S(2)}, u32[]{:S(2)}) %collective-permute-start) | collective-permute-done | bytes 3145760 | tf_op jit(solution)/shard_map/ppermute | solution.py:19
  207.1 1.7 copy-done
  208.8 35.1 %shard_map.73 = bf16[256,2048]{1,0:T(8,128)(2,1)} custom-call(bf16[3,2048,256]{2,1,0:T(8,128)(2,1)} %copy-done, bf16[3,2048,256]{2,1,0:T(8,128)(2,1)} %copy-done, bf16[3,2048,1024]{2,1,0:T(8,128)(2,1)} %refs_2_.7, bf16[3,2048,1024]{2,1,0:T(8,128)(2,1)} %refs_2_.7, f32[3,7,2048]{2,1,0:T(8,128)} %convert_bitcast_fusion.refs_4_.refs_5_.refs_3_, ...), custom_call_target="tpu_custom_call" | custom-call | flops 163577856 | bytes 6291456 | tf_op jit(solution)/shard_map/pallas_call | solution.py:70
  243.9 16.9 %convolution_convert_fusion.2 = bf16[256,8192]{1,0:T(8,128)(2,1)} fusion(bf16[256,2048]{1,0:T(8,128)(2,1)} %shard_map.73, bf16[2048,8192]{1,0:T(8,128)(2,1)} %param.11), kind=kOutput, calls=%fused_computation.2 | convolution fusion | flops 8592031744 | bytes 38797312 | tf_op jit(solution)/shard_map/dot_general | solution.py:134
  260.8 0.0 reduce-scatter.5.cloned.1.call-update
  260.9 0.0 reduce-scatter.11.cloned.1.call-done.refs_2_
  260.9 2.2 shard_map.77.refs_3_
  263.1 4.0 %shard_map.78.refs_3_ = bf16[2048,1024]{1,0:T(8,128)(2,1)} custom-call(bf16[2048,1024]{1,0:T(8,128)(2,1)} %refs_0_.13, f32[1,2048]{1,0:T(1,128)} %bitcast.15, bf16[256,2048]{1,0:T(8,128)(2,1)} %reduce-scatter.9.cloned.1.call-done.refs_2_, bf16[2048,1024]{1,0:T(8,128)(2,1)} %shard_map.77.refs_3_), custom_call_target="tpu_custom_call", output_to_operand_aliasing={{}: (3, {})} | custom-call | flops 1048576 | bytes 3145728 | tf_op jit(solution)/shard_map/pallas_call | solution.py:109
  267.1 23.3 %reduce-scatter.7.cloned.1.call-done.refs_2_ = bf16[384,2048]{1,0:T(8,128)(2,1)} async-done(((bf16[384,8192]{1,0:T(8,128)(2,1)}), bf16[384,2048]{1,0:T(8,128)(2,1)}) %reduce-scatter.7.cloned.1.call-update) | async-done | bytes 1572880 | tf_op jit(solution)/shard_map/reduce_scatter | solution.py:135
  290.4 5.4 %shard_map.79.refs_3_ = bf16[2048,1024]{1,0:T(8,128)(2,1)} custom-call(bf16[2048,1024]{1,0:T(8,128)(2,1)} %refs_0_.13, f32[1,2048]{1,0:T(1,128)} %bitcast.16, bf16[384,2048]{1,0:T(8,128)(2,1)} %reduce-scatter.7.cloned.1.call-done.refs_2_, bf16[2048,1024]{1,0:T(8,128)(2,1)} %shard_map.78.refs_3_), custom_call_target="tpu_custom_call", output_to_operand_aliasing={{}: (3, {})} | custom-call | flops 1572864 | bytes 4718592 | tf_op jit(solution)/shard_map/pallas_call | solution.py:109
  295.8 74.0 %reduce-scatter.5.cloned.1.call-done.refs_2_ = bf16[256,2048]{1,0:T(8,128)(2,1)} async-done(((bf16[256,8192]{1,0:T(8,128)(2,1)}), bf16[256,2048]{1,0:T(8,128)(2,1)}) %reduce-scatter.5.cloned.1.call-update) | async-done | bytes 1048592 | tf_op jit(solution)/shard_map/reduce_scatter | solution.py:135
  369.9 4.0 %shard_map.80 = bf16[2048,1024]{1,0:T(8,128)(2,1)} custom-call(bf16[2048,1024]{1,0:T(8,128)(2,1)} %refs_0_.13, f32[1,2048]{1,0:T(1,128)} %bitcast.17, bf16[256,2048]{1,0:T(8,128)(2,1)} %reduce-scatter.5.cloned.1.call-done.refs_2_, bf16[2048,1024]{1,0:T(8,128)(2,1)} %shard_map.79.refs_3_), custom_call_target="tpu_custom_call", output_to_operand_aliasing={{}: (3, {})} | custom-call | flops 1048576 | bytes 3145728 | tf_op jit(solution)/shard_map/pallas_call | solution.py:109
  (3 shorter events, 0.0 us)
Async XLA Ops:
  6.5 254.3 %reduce-scatter.11.cloned.1.call-start = ((), (), s32[]{:S(2)}) async-start(), calls=%async_computation.7 | async-start | bytes 2621440 | tf_op jit(solution)/shard_map/reduce_scatter | solution.py:135
  46.4 216.7 %reduce-scatter.9.cloned.1.call-start = ((), (), s32[]{:S(2)}) async-start(), calls=%async_computation.6 | async-start | bytes 5242880 | tf_op jit(solution)/shard_map/reduce_scatter | solution.py:135
  98.6 191.8 %reduce-scatter.7.cloned.1.call-start = ((), (), s32[]{:S(2)}) async-start(), calls=%async_computation.5 | async-start | bytes 7864320 | tf_op jit(solution)/shard_map/reduce_scatter | solution.py:135
  167.1 202.8 %reduce-scatter.5.cloned.1.call-start = ((), (), s32[]{:S(2)}) async-start(), calls=%async_computation.4 | async-start | bytes 5242880 | tf_op jit(solution)/shard_map/reduce_scatter | solution.py:135
  169.2 37.9 %collective-permute-start = (bf16[3,2048,256]{2,1,0:T(8,128)(2,1)S(1)}, bf16[3,2048,256]{2,1,0:T(8,128)(2,1)S(1)}, u32[]{:S(2)}, u32[]{:S(2)}) collective-permute-start(bf16[3,2048,256]{2,1,0:T(8,128)(2,1)S(1)} %slice.9), channel_id=1, source_target_pairs={{0,4},{4,8},{8,12},{12,16},{16,20},{20,24},{24,28},{1,5},{5,9},{9,... | collective-permute-start | bytes 9437192 | tf_op jit(solution)/shard_map/ppermute | solution.py:19
  207.1 1.7 copy-start
Sparse Core Ops, SparseCore 0:
  46.5 42.6 reduce-scatter.10
  98.8 77.9 reduce-scatter.8
  179.1 111.2 reduce-scatter.6
  292.6 77.2 reduce-scatter.4
where the time goes:
time: 383 us; the launch traced here: 380 us
  Pallas kernels  151 us (39%)
  waiting for transfers between devices  131 us (34%)
  matrix products  71.6 us (19%)
  between operations  13.2 us (3%)
  local copies, waits for them, and re-layouts  5.14 us (1%)
  starting transfers between devices  4.46 us (1%)
    pallas_call x4, Pallas kernels, features(): pl.pallas_call(functools.partial(feature_kernel, blocks), grid=(channels...  136 us
    reduce_scatter x4, waiting for transfers between devices, shards(): proj = lax.psum_scatter(part, 'mp', scatter_dimension=1, tiled=True)  97.4 us
    dot_general x4, matrix products, shards(): part = jnp.dot(y, w_out, preferred_element_type=F32).astype(BF16)  71.6 us
    ppermute x1, waiting for transfers between devices, from_behind(): lax.ppermute(value, axis, [(source, source + steps) for source in range(c...  33.9 us
    pallas_call x4, Pallas kernels, finish(): pl.pallas_call(finish_kernel, grid=(tokens // LANES, channels // rows), i...  15.6 us
  transfers between devices with their start and end apart: 5, of which 3 were waited for; matrix products, arithmetic and copies ran while one was open for 15% of the time, Pallas kernels for 34%

commit v1 on v0

--- a/solution.py
+++ b/solution.py
@@ -12,6 +12,7 @@
 LANES = 128
 F32 = jnp.float32
 BF16 = jnp.bfloat16
+MESH = pl.DeviceIdType.MESH
 
 
 def from_behind(value, axis, steps):
@@ -139,9 +140,495 @@
     return out
 
 
+PHASE = MTAPS // 4
+EDGE = 8
+COLS = 512
+VMEM_LIMIT = 62 << 20
+FEATURES = ((896, 128), (768, 128), (512, 256), (256, 256), (0, 256))
+PARTS = ((896, 128), (768, 128), (512, 256), (256, 256), (128, 128), (0, 128))
+PLANE = (2, 4, 6)
+SUM_IN, Y_IN, ACROSS_OUTER, ACROSS_INNER, SUM_OUT = range(5)
+
+
+def nine_taps(medium):
+    phase = [medium[i::4] for i in range(4)]
+    even = [phase[0], phase[2], phase[0] + phase[2]]
+    odd = [phase[1], phase[3], phase[1] + phase[3]]
+    return jnp.concatenate(even + odd + [a + b for a, b in zip(even, odd)], 0)
+
+
+def filtered(blocks, short_ref, nine_ref, lanes, wide, kv, xs, back, med):
+    count = (blocks - 2) * LANES // 4
+    held = (blocks - 1) * LANES // 4
+
+    def short(s, row):
+        total = short_ref[s, 0:1, lanes] * wide[s, row : row + LANES]
+        for j in range(1, STAPS):
+            total = total + short_ref[s, j : j + 1, lanes] * wide[s, row - j : row - j + LANES]
+        return total
+
+    for at in range(1, blocks):
+        row = at * LANES
+        kv[row - LANES : row] = (short(1, row) * short(2, row)).astype(BF16).astype(F32)
+    phase = [kv[pl.ds(p, held, stride=4)] for p in range(4)]
+    even = [phase[0], phase[2], phase[0] + phase[2]]
+    odd = [phase[1], phase[3], phase[1] + phase[3]]
+    for i, x in enumerate(even + odd + [a + b for a, b in zip(even, odd)]):
+        xs[i, EDGE : EDGE + held] = x
+
+    def conv(i, edge):
+        size, total = count + edge, None
+        for low in range(8):
+            start = EDGE + 8 - edge - low
+            block = xs[i, start : start + size + PHASE - 8]
+            for high in range(0, PHASE, 8):
+                first = PHASE - 8 - high
+                tap = i * PHASE + high + low
+                term = nine_ref[tap : tap + 1, lanes] * block[first : first + size]
+                total = term if total is None else total + term
+        return total
+
+    def delayed(value):
+        back[0 : count + EDGE] = value
+        return back[EDGE - 1 : EDGE - 1 + count]
+
+    def pair(g, edge):
+        first, second, both = conv(3 * g, edge), conv(3 * g + 1, EDGE), conv(3 * g + 2, edge)
+        return first[edge:] + delayed(second), both - first - second[EDGE - edge :]
+
+    odd0, odd1 = pair(1, EDGE)
+    late, odd1 = delayed(odd1), odd1[EDGE:]
+    even0, even1 = pair(0, 0)
+    both0, both1 = pair(2, 0)
+    med[pl.ds(0, count, stride=4)] = even0 + late
+    med[pl.ds(1, count, stride=4)] = both0 - even0 - odd0
+    med[pl.ds(2, count, stride=4)] = even1 + odd0
+    med[pl.ds(3, count, stride=4)] = both1 - even1 - odd1
+    for at in range(blocks - 2):
+        row = at * LANES
+        yield row, (short(0, row + 2 * LANES) * med[row : row + LANES]).astype(BF16)
+
+
+def line_kernel(
+    qkv, w_out, resid, short_ref, nine_ref, steer_ref,
+    out, wx_far, wx_near, rim,
+    y, yx, st1, st2, st3, r1, rp, rq, wbuf, qbuf, rbuf, wide, kv, xs, back, med,
+    send, recv, w_send, w_recv, rim_send, rim_recv, fetch_sem, q_sem, r_sem,
+):
+    s, m = lax.axis_index("seq"), lax.axis_index("mp")
+    channels, slab = qkv.shape[1], qkv.shape[2]
+    width = resid.shape[0]
+    steps = width // COLS
+    low = m < 2
+    inner = jnp.logical_or(m == 1, m == 2)
+    outer = jnp.logical_not(inner)
+    far_outer, far_inner = jnp.where(low, 3, 0), jnp.where(low, 2, 1)
+    near_inner, near_outer = jnp.where(low, 1, 2), jnp.where(low, 0, 3)
+    inward = (s, near_inner)
+    outward = (s, near_outer)
+    opposite = (s, jnp.where(low, 2, 1))
+
+    barrier = pltpu.get_barrier_semaphore()
+
+    def greet(condition, device):
+        @pl.when(condition)
+        def _():
+            pl.semaphore_signal(barrier, inc=1, device_id=device, device_id_type=MESH)
+
+    greet(m < 3, (s, jnp.minimum(m + 1, 3)))
+    greet(m > 0, (s, jnp.maximum(m - 1, 0)))
+    greet(s < 7, (jnp.minimum(s + 1, 7), m))
+    greet(s > 0, (jnp.maximum(s - 1, 0), m))
+    for flip in (1, *PLANE):
+        pl.semaphore_signal(barrier, inc=1, device_id=(s ^ flip, m), device_id_type=MESH)
+    one = lambda c: jnp.where(c, 1, 0)
+    pl.semaphore_wait(barrier, 4 + one(m < 3) + one(m > 0) + one(s < 7) + one(s > 0))
+
+    def remote(src, dst, sent, got, device):
+        return pltpu.make_async_remote_copy(
+            src_ref=src, dst_ref=dst, send_sem=sent, recv_sem=got, device_id=device, device_id_type=MESH
+        )
+
+    rim_copy = remote(qkv.at[:, :, slab - 256 : slab], rim, rim_send, rim_recv, (jnp.minimum(s + 1, 7), m))
+    pl.when(s < 7)(rim_copy.start)
+
+    share = channels // 8
+    held = (wx_far, wx_near)
+
+    def rows_of(device):
+        return pl.ds(pl.multiple_of(device * share, share), share)
+
+    def w_inward(g):
+        group = (far_inner, near_inner)[g]
+        columns = pl.ds(pl.multiple_of(group * width, width), width)
+        return remote(
+            w_out.at[rows_of(s), columns], held[g].at[rows_of(s)], w_send.at[g, 0], w_recv.at[g, 0], inward
+        )
+
+    def w_plane(g, i):
+        mine = held[g].at[rows_of(s)]
+        return remote(mine, mine, w_send.at[g, 1 + i], w_recv.at[g, 1 + i], (s ^ PLANE[i], m))
+
+    def w_core(g, i):
+        piece = held[g].at[rows_of(s if i == 0 else s ^ PLANE[i - 1])]
+        return remote(piece, piece, w_send.at[g, 4 + i], w_recv.at[g, 4 + i], (s ^ 1, m))
+
+    def relay_plane(g):
+        w_inward(g).wait_recv()
+        for i in range(3):
+            w_plane(g, i).start()
+        w_core(g, 0).start()
+
+    def relay_core(g):
+        for i in range(3):
+            w_plane(g, i).wait_recv()
+            w_core(g, 1 + i).start()
+
+    def relay_end(g):
+        for i in range(4):
+            w_core(g, i).wait_recv()
+
+    def rows(k):
+        return pl.ds(PARTS[k][0], PARTS[k][1])
+
+    def moving(kind, k):
+        src, dst, device = {
+            SUM_IN: (st1, r1, inward),
+            Y_IN: (y, yx, inward),
+            ACROSS_OUTER: (st1, rp, opposite),
+            ACROSS_INNER: (st2, rq, opposite),
+            SUM_OUT: (st3, r1, outward),
+        }[kind]
+        return remote(src.at[rows(k)], dst.at[rows(k)], send.at[kind, k], recv.at[kind, k], device)
+
+    def fetch(which, half, j):
+        if which in (0, 1):
+            block = held[which].at[:, pl.ds(pl.multiple_of(j * COLS, COLS), COLS)]
+        else:
+            group = {"fo": far_outer, "fi": far_inner, "ni": near_inner, "no": near_outer}[which]
+            block = w_out.at[:, pl.ds(pl.multiple_of(group * width + j * COLS, COLS), COLS)]
+        return pltpu.make_async_copy(block, wbuf.at[half, j], fetch_sem.at[half, j])
+
+    class Plan:
+        def __init__(self, units):
+            self.units, self.at, self.ended = units, 0, set()
+
+        def load(self, i):
+            if i < len(self.units):
+                which = self.units[i]
+                if which in (0, 1) and which not in self.ended:
+                    self.ended.add(which)
+                    relay_end(which)
+                for j in range(steps):
+                    fetch(which, i % 2, j).start()
+
+        def run(self, src, parts, each):
+            i = self.at
+            self.at += 1
+            self.load(i + 1)
+            first = PARTS[parts[-1]][0]
+            tokens = sum(PARTS[k][1] for k in parts)
+
+            def body(j, carry):
+                fetch(self.units[i], i % 2, j).wait()
+                total = jnp.dot(src[first : first + tokens], wbuf[i % 2, j], preferred_element_type=F32)
+                each(total, j, pl.ds(first, tokens), pl.ds(pl.multiple_of(j * COLS, COLS), COLS))
+                return carry
+
+            lax.fori_loop(0, steps, body, 0)
+
+    def put(dst, *adds):
+        def each(total, j, at, columns):
+            for ref in adds:
+                total = total + ref[at, columns].astype(F32)
+            dst[at, columns] = total.astype(BF16)
+
+        return each
+
+    def resid_in(slot, first, tokens):
+        return pltpu.make_async_copy(
+            resid.at[:, first : first + tokens], rbuf.at[slot, :, 0:tokens], r_sem.at[0, slot]
+        )
+
+    def out_of(slot, first, tokens):
+        return pltpu.make_async_copy(
+            rbuf.at[slot, :, 0:tokens], out.at[:, first : first + tokens], r_sem.at[1, slot]
+        )
+
+    leaving = []
+
+    def final(plan, src, parts, ref):
+        first = PARTS[parts[-1]][0]
+        tokens = sum(PARTS[k][1] for k in parts)
+        slot = len(leaving) % 2
+        if len(leaving) >= 2:
+            out_of(*leaving[-2]).wait()
+        resid_in(slot, first, tokens).start()
+        leaving.append((slot, first, tokens))
+
+        def each(total, j, at, columns):
+            @pl.when(j == 0)
+            def _():
+                resid_in(slot, first, tokens).wait()
+
+            total = total + ref[at, columns].astype(F32) + steer_ref[0:1, columns]
+            rbuf[slot, columns, 0:tokens] = (
+                rbuf[slot, columns, 0:tokens].astype(F32) + total.T
+            ).astype(BF16)
+
+        plan.run(src, parts, each)
+        out_of(slot, first, tokens).start()
+
+    def settle():
+        for left in leaving[-2:]:
+            out_of(*left).wait()
+        leaving.clear()
+
+    def feature(k):
+        first, tokens = FEATURES[k]
+        span = tokens + 256
+
+        def load(c, slot, act):
+            lanes = pl.ds(pl.multiple_of(c * LANES, LANES), LANES)
+            if first > 0:
+                act(pltpu.make_async_copy(
+                    qkv.at[:, lanes, first - 256 : first + tokens], qbuf.at[slot, :, :, 0:span], q_sem.at[0, slot]
+                ))
+            else:
+                act(pltpu.make_async_copy(
+                    qkv.at[:, lanes, 0:tokens], qbuf.at[slot, :, :, 256:span], q_sem.at[0, slot]
+                ))
+
+                @pl.when(s > 0)
+                def _():
+                    act(pltpu.make_async_copy(rim.at[:, lanes], qbuf.at[slot, :, :, 0:256], q_sem.at[1, slot]))
+
+        if first == 0:
+
+            @pl.when(s > 0)
+            def _():
+                rim_copy.wait_recv()
+
+            @pl.when(s == 0)
+            def _():
+                qbuf[:, :, :, 0:256] = jnp.zeros((2, 3, LANES, 256), BF16)
+
+        load(0, 0, lambda copy: copy.start())
+        count = channels // LANES
+
+        def body(c, carry):
+            slot = lax.rem(c, 2)
+
+            @pl.when(c + 1 < count)
+            def _():
+                load(c + 1, 1 - slot, lambda copy: copy.start())
+
+            load(c, slot, lambda copy: copy.wait())
+            lanes = pl.ds(pl.multiple_of(c * LANES, LANES), LANES)
+            for at in range(span // LANES):
+                for i in range(3):
+                    if i > 0 or at > 0:
+                        wide[i, at * LANES : (at + 1) * LANES] = (
+                            qbuf[slot, i, :, at * LANES : (at + 1) * LANES].astype(F32).T
+                        )
+            for row, value in filtered(span // LANES, short_ref, nine_ref, lanes, wide, kv, xs, back, med):
+                y[first + row : first + row + LANES, lanes] = value
+            return carry
+
+        lax.fori_loop(0, count, body, 0)
+
+    def wait_in(kind, *parts):
+        for k in parts:
+            moving(kind, k).wait_recv()
+
+    def go(kind, *parts):
+        for k in parts:
+            moving(kind, k).start()
+
+    class Inner:
+        def __init__(self, plan):
+            self.plan = plan
+
+        def cross(self, *parts):
+            wait_in(SUM_IN, *parts)
+            self.plan.run(y, parts, put(st1, r1))
+            go(ACROSS_OUTER, *parts)
+
+        def far(self, *parts):
+            self.plan.run(y, parts, put(st2))
+
+        def far_end(self, *parts):
+            wait_in(Y_IN, *parts)
+            self.plan.run(yx, parts, put(st2, st2))
+            go(ACROSS_INNER, *parts)
+
+        def out(self, *parts):
+            wait_in(ACROSS_OUTER, *parts)
+            self.plan.run(y, parts, put(st3, rp))
+            go(SUM_OUT, *parts)
+
+        def near(self, *parts):
+            wait_in(ACROSS_INNER, *parts)
+            self.plan.run(y, parts, put(rq, rq))
+
+        def end(self, *parts):
+            final(self.plan, yx, parts, rq)
+
+    UNIT = {"cross": "fo", "far": "fi", "far_end": 0, "out": "no", "near": "ni", "end": 1}
+    inner_steps = INNER_STEPS
+    inner_plan = Plan([UNIT[step[0]] for block in inner_steps for step in block if step[0] in UNIT])
+    inner_work = Inner(inner_plan)
+
+    class Outer:
+        def __init__(self, plan):
+            self.plan = plan
+
+        def sum(self, *parts):
+            self.plan.run(y, parts, put(st1))
+
+        def go_sum(self, *parts):
+            go(SUM_IN, *parts)
+
+        def go_y(self, *parts):
+            go(Y_IN, *parts)
+
+        def go_w(self, g):
+            w_inward(g).start()
+
+        def end(self, *parts):
+            wait_in(SUM_OUT, *parts)
+            final(self.plan, y, parts, r1)
+
+    OUTER_UNIT = {"sum": "fo", "end": "no"}
+    outer_steps = OUTER_STEPS
+    outer_plan = Plan([OUTER_UNIT[step[0]] for block in outer_steps for step in block if step[0] in OUTER_UNIT])
+    outer_work = Outer(outer_plan)
+
+    @pl.when(outer)
+    def _():
+        w_inward(0).start()
+        outer_plan.load(0)
+
+    @pl.when(inner)
+    def _():
+        inner_plan.load(0)
+
+    for k in range(len(FEATURES)):
+        feature(k)
+
+        @pl.when(inner)
+        def _():
+            for step in inner_steps[k]:
+                if step[0] == "plane":
+                    relay_plane(step[1])
+                elif step[0] == "core":
+                    relay_core(step[1])
+                else:
+                    getattr(inner_work, step[0])(*step[1:])
+            if k == len(FEATURES) - 1:
+                settle()
+                for part in range(len(PARTS)):
+                    moving(ACROSS_OUTER, part).wait_send()
+                    moving(ACROSS_INNER, part).wait_send()
+                    moving(SUM_OUT, part).wait_send()
+                for g in range(2):
+                    for i in range(3):
+                        w_plane(g, i).wait_send()
+                    for i in range(4):
+                        w_core(g, i).wait_send()
+
+        @pl.when(outer)
+        def _():
+            for step in outer_steps[k]:
+                getattr(outer_work, step[0])(*step[1:])
+            if k == len(FEATURES) - 1:
+                settle()
+                for part in range(len(PARTS)):
+                    moving(SUM_IN, part).wait_send()
+                    moving(Y_IN, part).wait_send()
+                for g in range(2):
+                    w_inward(g).wait_send()
+
+    pl.when(s < 7)(rim_copy.wait_send)
+
+
+INNER_STEPS = (
+    (),
+    (("plane", 0), ("cross", 0)),
+    (("cross", 1),),
+    (("core", 0), ("cross", 2), ("far", 0, 1), ("far_end", 0, 1), ("out", 0, 1)),
+    (
+        ("cross", 3), ("out", 2), ("plane", 1), ("cross", 4), ("out", 3), ("far", 2), ("core", 1), ("cross", 5),
+        ("far_end", 2), ("out", 4, 5), ("near", 0, 1), ("end", 0, 1), ("far", 3), ("far_end", 3), ("near", 2), ("end", 2),
+        ("far", 4, 5), ("far_end", 4), ("near", 3), ("end", 3), ("far_end", 5), ("near", 4, 5), ("end", 4, 5),
+    ),
+)
+OUTER_STEPS = (
+    (("sum", 0), ("go_sum", 0)),
+    (("sum", 1), ("go_sum", 1), ("go_y", 0, 1)),
+    (("sum", 2), ("go_sum", 2)),
+    (("sum", 3), ("go_sum", 3), ("go_w", 1)),
+    (
+        ("sum", 4, 5), ("go_sum", 4), ("go_y", 2), ("go_sum", 5), ("go_y", 3, 4, 5),
+        ("end", 0, 1), ("end", 2), ("end", 3), ("end", 4, 5),
+    ),
+)
+
+
+def lined(qkv, short_taps, medium_taps, skip_gain, w_out, resid, steer):
+    channels, slab = qkv.shape[1:]
+    width = resid.shape[0]
+    short = jnp.swapaxes(short_taps.astype(F32), 1, 2)
+    medium = medium_taps.astype(F32)
+    medium = jnp.concatenate([medium[:, :1] + skip_gain[:, None], medium[:, 1:]], 1).T
+    whole = pl.BlockSpec(memory_space=pltpu.VMEM)
+    anywhere = pl.BlockSpec(memory_space=pl.ANY)
+    token = lambda: pltpu.VMEM((slab, channels), BF16)
+    dma = pltpu.SemaphoreType.DMA
+    span = 512
+    return pl.pallas_call(
+        line_kernel,
+        in_specs=[anywhere] * 3 + [whole] * 3,
+        out_specs=[anywhere] * 4,
+        out_shape=[
+            jax.ShapeDtypeStruct(resid.shape, BF16),
+            jax.ShapeDtypeStruct((channels, width), BF16),
+            jax.ShapeDtypeStruct((channels, width), BF16),
+            jax.ShapeDtypeStruct((3, channels, 256), BF16),
+        ],
+        scratch_shapes=[token() for _ in range(8)]
+        + [
+            pltpu.VMEM((2, width // COLS, channels, COLS), BF16),
+            pltpu.VMEM((2, 3, LANES, span), BF16),
+            pltpu.VMEM((2, width, 256), BF16),
+            pltpu.VMEM((3, span, LANES), F32),
+            pltpu.VMEM((span - LANES, LANES), F32),
+            pltpu.VMEM((9, EDGE + (span - LANES) // 4, LANES), F32),
+            pltpu.VMEM((EDGE + 64, LANES), F32),
+            pltpu.VMEM((256, LANES), F32),
+            dma((5, len(PARTS))),
+            dma((5, len(PARTS))),
+            dma((2, 8)),
+            dma((2, 8)),
+            dma,
+            dma,
+            dma((2, width // COLS)),
+            dma((2, 2)),
+            dma((2, 2)),
+        ],
+        compiler_params=pltpu.CompilerParams(
+            collective_id=0, has_side_effects=True, vmem_limit_bytes=VMEM_LIMIT
+        ),
+        cost_estimate=pl.CostEstimate(
+            flops=12 * channels * slab * width, bytes_accessed=20 * channels * width, transcendentals=0
+        ),
+    )(qkv, w_out, resid, short, nine_taps(medium), steer[None])[0]
+
+
 def solution(mesh):
+    line = mesh.shape["mp"] == 4 and mesh.shape["seq"] == 8
     return jax.shard_map(
-        shards,
+        lined if line else shards,
         mesh=mesh,
         in_specs=(
             P(None, "mp", "seq"),

time: 383 us -> 304 us (0.79)
  Pallas kernels: 151 us -> 285 us
  waiting for transfers between devices: 131 us -> 0 us
  matrix products: 71.6 us -> 0 us
  between operations: 13.2 us -> 0.09 us
  local copies, waits for them, and re-layouts: 5.14 us -> 9.77 us
  starting transfers between devices: 4.46 us -> 0 us
    pallas_call x8 -> x1, Pallas kernels: 151 us -> 285 us  [lined(): pl.pallas_call(line_kernel, in_specs=[anywhere] * 3 + [whole] * 3, out_sp...]
    reduce_scatter x4 -> x0, waiting for transfers between devices: 97.4 us -> none  [shards(): proj = lax.psum_scatter(part, 'mp', scatter_dimension=1, tiled=True)]
    dot_general x4 -> x0, matrix products: 71.6 us -> none  [shards(): part = jnp.dot(y, w_out, preferred_element_type=F32).astype(BF16)]
    ppermute x1 -> x0, waiting for transfers between devices: 33.9 us -> none  [from_behind(): lax.ppermute(value, axis, [(source, source + steps) for source in range(c...]
    unnamed x3 -> x8, local copies, waits for them, and re-layouts: 2.91 us -> 8.78 us
    ppermute x1 -> x0, starting transfers between devices: 3.93 us -> none  [from_behind(): lax.ppermute(value, axis, [(source, source + steps) for source in range(c...]
  transfers between devices with their start and end apart: 5 -> 0, of which waited for: 3 -> 0; matrix products, arithmetic and copies ran while one was open for 15% -> 0% of each run, Pallas kernels for 34% -> 0%
where the time goes in v1:
time: 304 us; the launch traced here: 300 us
  Pallas kernels  285 us (94%)
  local copies, waits for them, and re-layouts  9.77 us (3%)
  other arithmetic  5.45 us (2%)
    pallas_call x1, Pallas kernels, lined(): pl.pallas_call(line_kernel, in_specs=[anywhere] * 3 + [whole] * 3, out_sp...  285 us
    unnamed x8, local copies, waits for them, and re-layouts  8.78 us

profile of v1, /device:TPU:9, one launch (start us, length us, event | category | flops | bytes accessed | tf_op | source)
XLA Modules:
  0.0 300.4 jit_solution(14378229245963966376)
XLA Ops:
  0.0 1.6 convert_bitcast_fusion.short_ref
  1.6 0.0 copy-start
  1.6 1.3 copy.8
  2.8 0.1 slice.25
  3.0 0.1 convert_element_type.4
  3.1 0.0 copy-done
  3.1 0.1 maximum_bitcast_fusion
  3.2 0.2 slice.23
  3.4 0.2 slice.22
  3.7 0.2 slice.21
  3.9 0.2 slice.20
  4.1 0.7 constant_dynamic-update-slice_fusion.3
  4.8 0.7 constant_dynamic-update-slice_fusion.2
  5.5 0.7 add_dynamic-update-slice_fusion.4
  6.3 0.7 constant_dynamic-update-slice_fusion.1
  7.0 0.7 constant_dynamic-update-slice_fusion
  7.7 0.7 add_dynamic-update-slice_fusion.3
  8.4 0.7 add_dynamic-update-slice_fusion.2
  9.2 0.7 add_dynamic-update-slice_fusion.1
  9.9 0.8 add_dynamic-update-slice_fusion.nine_ref
  10.7 285.1 %shard_map.73 = (bf16[2048,1024]{1,0:T(8,128)(2,1)}, bf16[2048,2048]{1,0:T(8,128)(2,1)}, bf16[2048,2048]{1,0:T(8,128)(2,1)}, bf16[3,2048,256]{2,1,0:T(8,128)(2,1)}) custom-call(bf16[3,2048,1024]{2,1,0:T(8,128)(2,1)} %qkv.1, bf16[2048,8192]{1,0:T(8,128)(2,1)} %w_out.1, bf16[2048,1024]{1,0:T(8,128)(2,1)} %resid.1, ...), custom_call_target="tpu_custom_call" | custom-call | flops 51539607552 | bytes 83886080 | tf_op jit(solution)/shard_map/pallas_call | solution.py:589
  295.8 4.6 %copy.18 = bf16[2048,1024]{1,0:T(8,128)(2,1)} copy(bf16[2048,1024]{1,0:T(8,128)(2,1)} %get-tuple-element.6) | data formatting | bytes 8388608
  (1 shorter events, 0.0 us)
Async XLA Ops:
  1.6 1.5 copy-start

commit v2 on v1

--- a/solution.py
+++ b/solution.py
@@ -145,19 +145,22 @@
 COLS = 512
 VMEM_LIMIT = 62 << 20
 FEATURES = ((896, 128), (768, 128), (512, 256), (256, 256), (0, 256))
-PARTS = ((896, 128), (768, 128), (512, 256), (256, 256), (128, 128), (0, 128))
+PARTS = ((896, 128), (768, 128), (512, 256), (256, 256), (128, 128), (64, 64), (0, 64))
 PLANE = (2, 4, 6)
 SUM_IN, Y_IN, ACROSS_OUTER, ACROSS_INNER, SUM_OUT = range(5)
 
 
-def nine_taps(medium):
-    phase = [medium[i::4] for i in range(4)]
+def split_taps(c, lanes, medium_ref, skip_ref, nine, spare):
+    spare[0:MTAPS] = medium_ref[pl.ds(pl.multiple_of(c * LANES, LANES), LANES)].astype(F32).T
+    spare[0:1] = spare[0:1] + skip_ref[0:1, lanes]
+    phase = [spare[pl.ds(p, PHASE, stride=4)] for p in range(4)]
     even = [phase[0], phase[2], phase[0] + phase[2]]
     odd = [phase[1], phase[3], phase[1] + phase[3]]
-    return jnp.concatenate(even + odd + [a + b for a, b in zip(even, odd)], 0)
-
-
-def filtered(blocks, short_ref, nine_ref, lanes, wide, kv, xs, back, med):
+    for i, x in enumerate(even + odd + [a + b for a, b in zip(even, odd)]):
+        nine[i * PHASE : (i + 1) * PHASE, lanes] = x
+
+
+def filtered(blocks, known, kept, short_ref, nine_ref, top, lanes, wide, kv, xs, back, med):
     count = (blocks - 2) * LANES // 4
     held = (blocks - 1) * LANES // 4
 
@@ -167,9 +170,13 @@
             total = total + short_ref[s, j : j + 1, lanes] * wide[s, row - j : row - j + LANES]
         return total
 
-    for at in range(1, blocks):
+    for at in range(1, blocks - 1 if known else blocks):
         row = at * LANES
         kv[row - LANES : row] = (short(1, row) * short(2, row)).astype(BF16).astype(F32)
+    if known:
+        kv[(blocks - 2) * LANES : (blocks - 1) * LANES] = top[:, lanes]
+    if kept:
+        top[:, lanes] = kv[0:LANES]
     phase = [kv[pl.ds(p, held, stride=4)] for p in range(4)]
     even = [phase[0], phase[2], phase[0] + phase[2]]
     odd = [phase[1], phase[3], phase[1] + phase[3]]
@@ -210,9 +217,9 @@
 
 
 def line_kernel(
-    qkv, w_out, resid, short_ref, nine_ref, steer_ref,
+    qkv, w_out, resid, short_taps, medium_ref, skip_ref, steer_ref,
     out, wx_far, wx_near, rim,
-    y, yx, st1, st2, st3, r1, rp, rq, wbuf, qbuf, rbuf, wide, kv, xs, back, med,
+    y, yx, st1, st2, st3, r1, rp, rq, wbuf, qbuf, rbuf, short_ref, nine_ref, top, wide, kv, xs, back, med,
     send, recv, w_send, w_recv, rim_send, rim_recv, fetch_sem, q_sem, r_sem,
 ):
     s, m = lax.axis_index("seq"), lax.axis_index("mp")
@@ -252,41 +259,42 @@
     rim_copy = remote(qkv.at[:, :, slab - 256 : slab], rim, rim_send, rim_recv, (jnp.minimum(s + 1, 7), m))
     pl.when(s < 7)(rim_copy.start)
 
-    share = channels // 8
+    share = channels // 16
     held = (wx_far, wx_near)
 
-    def rows_of(device):
-        return pl.ds(pl.multiple_of(device * share, share), share)
-
-    def w_inward(g):
+    def rows_of(device, h):
+        return pl.ds(pl.multiple_of((device * 2 + h) * share, share), share)
+
+    def w_inward(g, h):
         group = (far_inner, near_inner)[g]
         columns = pl.ds(pl.multiple_of(group * width, width), width)
         return remote(
-            w_out.at[rows_of(s), columns], held[g].at[rows_of(s)], w_send.at[g, 0], w_recv.at[g, 0], inward
+            w_out.at[rows_of(s, h), columns], held[g].at[rows_of(s, h)], w_send.at[g, h, 0], w_recv.at[g, h, 0], inward
         )
 
-    def w_plane(g, i):
-        mine = held[g].at[rows_of(s)]
-        return remote(mine, mine, w_send.at[g, 1 + i], w_recv.at[g, 1 + i], (s ^ PLANE[i], m))
-
-    def w_core(g, i):
-        piece = held[g].at[rows_of(s if i == 0 else s ^ PLANE[i - 1])]
-        return remote(piece, piece, w_send.at[g, 4 + i], w_recv.at[g, 4 + i], (s ^ 1, m))
-
-    def relay_plane(g):
-        w_inward(g).wait_recv()
+    def w_plane(g, h, i):
+        mine = held[g].at[rows_of(s, h)]
+        return remote(mine, mine, w_send.at[g, h, 1 + i], w_recv.at[g, h, 1 + i], (s ^ PLANE[i], m))
+
+    def w_core(g, h, i):
+        piece = held[g].at[rows_of(s if i == 0 else s ^ PLANE[i - 1], h)]
+        return remote(piece, piece, w_send.at[g, h, 4 + i], w_recv.at[g, h, 4 + i], (s ^ 1, m))
+
+    def relay_plane(g, h):
+        w_inward(g, h).wait_recv()
         for i in range(3):
-            w_plane(g, i).start()
-        w_core(g, 0).start()
-
-    def relay_core(g):
+            w_plane(g, h, i).start()
+        w_core(g, h, 0).start()
+
+    def relay_core(g, h):
         for i in range(3):
-            w_plane(g, i).wait_recv()
-            w_core(g, 1 + i).start()
+            w_plane(g, h, i).wait_recv()
+            w_core(g, h, 1 + i).start()
 
     def relay_end(g):
-        for i in range(4):
-            w_core(g, i).wait_recv()
+        for h in range(2):
+            for i in range(4):
+                w_core(g, h, i).wait_recv()
 
     def rows(k):
         return pl.ds(PARTS[k][0], PARTS[k][1])
@@ -357,7 +365,7 @@
 
     leaving = []
 
-    def final(plan, src, parts, ref):
+    def final(kind, parts, left, right):
         first = PARTS[parts[-1]][0]
         tokens = sum(PARTS[k][1] for k in parts)
         slot = len(leaving) % 2
@@ -365,18 +373,17 @@
             out_of(*leaving[-2]).wait()
         resid_in(slot, first, tokens).start()
         leaving.append((slot, first, tokens))
-
-        def each(total, j, at, columns):
-            @pl.when(j == 0)
-            def _():
-                resid_in(slot, first, tokens).wait()
-
-            total = total + ref[at, columns].astype(F32) + steer_ref[0:1, columns]
-            rbuf[slot, columns, 0:tokens] = (
-                rbuf[slot, columns, 0:tokens].astype(F32) + total.T
-            ).astype(BF16)
-
-        plan.run(src, parts, each)
+        wait_in(kind, *parts)
+        resid_in(slot, first, tokens).wait()
+        at = pl.ds(first, tokens)
+
+        def body(j, carry):
+            columns = pl.ds(pl.multiple_of(j * COLS, COLS), COLS)
+            total = left[at, columns].astype(F32) + right[at, columns].astype(F32) + steer_ref[0:1, columns]
+            rbuf[slot, columns, 0:tokens] = (rbuf[slot, columns, 0:tokens].astype(F32) + total.T).astype(BF16)
+            return carry
+
+        lax.fori_loop(0, steps, body, 0)
         out_of(slot, first, tokens).start()
 
     def settle():
@@ -384,26 +391,27 @@
             out_of(*left).wait()
         leaving.clear()
 
-    def feature(k):
+    blocks_of_channels = channels // LANES
+
+    def load(k, c, slot, act):
         first, tokens = FEATURES[k]
         span = tokens + 256
-
-        def load(c, slot, act):
-            lanes = pl.ds(pl.multiple_of(c * LANES, LANES), LANES)
-            if first > 0:
-                act(pltpu.make_async_copy(
-                    qkv.at[:, lanes, first - 256 : first + tokens], qbuf.at[slot, :, :, 0:span], q_sem.at[0, slot]
-                ))
-            else:
-                act(pltpu.make_async_copy(
-                    qkv.at[:, lanes, 0:tokens], qbuf.at[slot, :, :, 256:span], q_sem.at[0, slot]
-                ))
-
-                @pl.when(s > 0)
-                def _():
-                    act(pltpu.make_async_copy(rim.at[:, lanes], qbuf.at[slot, :, :, 0:256], q_sem.at[1, slot]))
-
-        if first == 0:
+        lanes = pl.ds(pl.multiple_of(c * LANES, LANES), LANES)
+        if first > 0:
+            act(pltpu.make_async_copy(
+                qkv.at[:, lanes, first - 256 : first + tokens], qbuf.at[slot, :, :, 0:span], q_sem.at[0, slot]
+            ))
+        else:
+            act(pltpu.make_async_copy(
+                qkv.at[:, lanes, 0:tokens], qbuf.at[slot, :, :, 256:span], q_sem.at[0, slot]
+            ))
+
+            @pl.when(s > 0)
+            def _():
+                act(pltpu.make_async_copy(rim.at[:, lanes], qbuf.at[slot, :, :, 0:256], q_sem.at[1, slot]))
+
+    def begin(k):
+        if FEATURES[k][0] == 0:
 
             @pl.when(s > 0)
             def _():
@@ -413,29 +421,40 @@
             def _():
                 qbuf[:, :, :, 0:256] = jnp.zeros((2, 3, LANES, 256), BF16)
 
-        load(0, 0, lambda copy: copy.start())
-        count = channels // LANES
+        load(k, 0, 0, lambda copy: copy.start())
+
+    def feature(k, start, stop):
+        first, tokens = FEATURES[k]
+        blocks = (tokens + 256) // LANES
+        known, kept = k > 0, k + 1 < len(FEATURES)
 
         def body(c, carry):
             slot = lax.rem(c, 2)
 
-            @pl.when(c + 1 < count)
+            @pl.when(c + 1 < blocks_of_channels)
             def _():
-                load(c + 1, 1 - slot, lambda copy: copy.start())
-
-            load(c, slot, lambda copy: copy.wait())
+                load(k, c + 1, 1 - slot, lambda copy: copy.start())
+
+            load(k, c, slot, lambda copy: copy.wait())
             lanes = pl.ds(pl.multiple_of(c * LANES, LANES), LANES)
-            for at in range(span // LANES):
+            if k == 0:
+                split_taps(c, lanes, medium_ref, skip_ref, nine_ref, med)
+            for at in range(blocks):
                 for i in range(3):
-                    if i > 0 or at > 0:
+                    if at > 0 if i == 0 else not (known and at == blocks - 1):
                         wide[i, at * LANES : (at + 1) * LANES] = (
                             qbuf[slot, i, :, at * LANES : (at + 1) * LANES].astype(F32).T
                         )
-            for row, value in filtered(span // LANES, short_ref, nine_ref, lanes, wide, kv, xs, back, med):
+            pieces = filtered(
+                blocks, known, kept, short_ref, nine_ref, top, lanes, wide, kv, xs, back, med
+            )
+            for row, value in pieces:
                 y[first + row : first + row + LANES, lanes] = value
             return carry
 
-        lax.fori_loop(0, count, body, 0)
+        lax.fori_loop(start, stop, body, 0)
+        if stop == blocks_of_channels and k + 1 < len(FEATURES):
+            begin(k + 1)
 
     def wait_in(kind, *parts):
         for k in parts:
@@ -468,15 +487,16 @@
             go(SUM_OUT, *parts)
 
         def near(self, *parts):
-            wait_in(ACROSS_INNER, *parts)
-            self.plan.run(y, parts, put(rq, rq))
-
-        def end(self, *parts):
-            final(self.plan, yx, parts, rq)
-
-    UNIT = {"cross": "fo", "far": "fi", "far_end": 0, "out": "no", "near": "ni", "end": 1}
-    inner_steps = INNER_STEPS
-    inner_plan = Plan([UNIT[step[0]] for block in inner_steps for step in block if step[0] in UNIT])
+            self.plan.run(y, parts, put(r1))
+
+        def near_end(self, *parts):
+            self.plan.run(yx, parts, put(r1, r1))
+
+        def final(self, *parts):
+            final(ACROSS_INNER, parts, r1, rq)
+
+    UNIT = {"cross": "fo", "far": "fi", "far_end": 0, "out": "no", "near": "ni", "near_end": 1}
+    inner_plan = Plan([UNIT[step[0]] for entry in SCHEDULE for step in entry[3] if step[0] in UNIT])
     inner_work = Inner(inner_plan)
 
     class Outer:
@@ -493,94 +513,102 @@
             go(Y_IN, *parts)
 
         def go_w(self, g):
-            w_inward(g).start()
-
-        def end(self, *parts):
-            wait_in(SUM_OUT, *parts)
-            final(self.plan, y, parts, r1)
-
-    OUTER_UNIT = {"sum": "fo", "end": "no"}
-    outer_steps = OUTER_STEPS
-    outer_plan = Plan([OUTER_UNIT[step[0]] for block in outer_steps for step in block if step[0] in OUTER_UNIT])
+            for h in range(2):
+                w_inward(g, h).start()
+
+        def out(self, *parts):
+            self.plan.run(y, parts, put(rp))
+
+        def final(self, *parts):
+            final(SUM_OUT, parts, rp, r1)
+
+    OUTER_UNIT = {"sum": "fo", "out": "no"}
+    outer_plan = Plan([OUTER_UNIT[step[0]] for entry in SCHEDULE for step in entry[4] if step[0] in OUTER_UNIT])
     outer_work = Outer(outer_plan)
+
+    begin(0)
 
     @pl.when(outer)
     def _():
-        w_inward(0).start()
+        for h in range(2):
+            w_inward(0, h).start()
         outer_plan.load(0)
 
     @pl.when(inner)
     def _():
         inner_plan.load(0)
 
-    for k in range(len(FEATURES)):
-        feature(k)
+    short_ref[...] = short_taps[...].astype(F32)
+    for number, (k, start, stop, inner_steps, outer_steps) in enumerate(SCHEDULE):
+        feature(k, start, stop)
+        ending = number == len(SCHEDULE) - 1
 
         @pl.when(inner)
         def _():
-            for step in inner_steps[k]:
+            for step in inner_steps:
                 if step[0] == "plane":
-                    relay_plane(step[1])
+                    relay_plane(*step[1:])
                 elif step[0] == "core":
-                    relay_core(step[1])
+                    relay_core(*step[1:])
                 else:
                     getattr(inner_work, step[0])(*step[1:])
-            if k == len(FEATURES) - 1:
+            if ending:
                 settle()
                 for part in range(len(PARTS)):
                     moving(ACROSS_OUTER, part).wait_send()
                     moving(ACROSS_INNER, part).wait_send()
                     moving(SUM_OUT, part).wait_send()
                 for g in range(2):
-                    for i in range(3):
-                        w_plane(g, i).wait_send()
-                    for i in range(4):
-                        w_core(g, i).wait_send()
+                    for h in range(2):
+                        for i in range(3):
+                            w_plane(g, h, i).wait_send()
+                        for i in range(4):
+                            w_core(g, h, i).wait_send()
 
         @pl.when(outer)
         def _():
-            for step in outer_steps[k]:
+            for step in outer_steps:
                 getattr(outer_work, step[0])(*step[1:])
-            if k == len(FEATURES) - 1:
+            if ending:
                 settle()
                 for part in range(len(PARTS)):
                     moving(SUM_IN, part).wait_send()
                     moving(Y_IN, part).wait_send()
                 for g in range(2):
-                    w_inward(g).wait_send()
+                    for h in range(2):
+                        w_inward(g, h).wait_send()
 
     pl.when(s < 7)(rim_copy.wait_send)
 
 
-INNER_STEPS = (
-    (),
-    (("plane", 0), ("cross", 0)),
-    (("cross", 1),),
-    (("core", 0), ("cross", 2), ("far", 0, 1), ("far_end", 0, 1), ("out", 0, 1)),
-    (
-        ("cross", 3), ("out", 2), ("plane", 1), ("cross", 4), ("out", 3), ("far", 2), ("core", 1), ("cross", 5),
-        ("far_end", 2), ("out", 4, 5), ("near", 0, 1), ("end", 0, 1), ("far", 3), ("far_end", 3), ("near", 2), ("end", 2),
-        ("far", 4, 5), ("far_end", 4), ("near", 3), ("end", 3), ("far_end", 5), ("near", 4, 5), ("end", 4, 5),
-    ),
-)
-OUTER_STEPS = (
-    (("sum", 0), ("go_sum", 0)),
-    (("sum", 1), ("go_sum", 1), ("go_y", 0, 1)),
-    (("sum", 2), ("go_sum", 2)),
-    (("sum", 3), ("go_sum", 3), ("go_w", 1)),
-    (
-        ("sum", 4, 5), ("go_sum", 4), ("go_y", 2), ("go_sum", 5), ("go_y", 3, 4, 5),
-        ("end", 0, 1), ("end", 2), ("end", 3), ("end", 4, 5),
-    ),
+SCHEDULE = (
+    (0, 0, 11, (("plane", 0, 0),), ()),
+    (0, 11, 16, (), (("sum", 0), ("go_sum", 0))),
+    (1, 0, 8, (("plane", 0, 1),), ()),
+    (1, 8, 16, (), (("sum", 1), ("go_sum", 1), ("go_y", 0, 1))),
+    (2, 0, 4, (("cross", 0),), ()),
+    (2, 4, 11, (("core", 0, 0), ("cross", 1)), ()),
+    (2, 11, 16, (("core", 0, 1), ("far", 0, 1), ("far_end", 0)), (("sum", 2), ("go_sum", 2))),
+    (3, 0, 8, (("far_end", 1), ("out", 0, 1)), ()),
+    (3, 8, 16, (("cross", 2),), (("sum", 3), ("go_sum", 3))),
+    (4, 0, 14, (("cross", 3),), ()),
+    (4, 14, 16, (
+        ("near", 0, 1), ("out", 2), ("near", 2), ("plane", 1, 0), ("cross", 4), ("plane", 1, 1),
+        ("far", 2), ("far_end", 2), ("core", 1, 0), ("cross", 5), ("cross", 6), ("core", 1, 1), ("out", 3), ("near", 3),
+        ("far", 3), ("far_end", 3), ("out", 4, 5, 6), ("far", 4, 5, 6), ("far_end", 4), ("near", 4, 5, 6), ("far_end", 5), ("near_end", 0, 1), ("far_end", 6),
+        ("near_end", 2), ("near_end", 3), ("near_end", 4, 5, 6), ("final", 0, 1), ("final", 2),
+        ("final", 3), ("final", 4), ("final", 5, 6),
+    ), (
+        ("sum", 4, 5, 6), ("go_sum", 4), ("go_w", 1), ("go_y", 2), ("go_sum", 5, 6), ("go_y", 3, 4, 5, 6),
+        ("out", 0, 1), ("out", 2), ("out", 3), ("out", 4, 5, 6),
+        ("final", 0, 1), ("final", 2), ("final", 3), ("final", 4, 5, 6),
+    )),
 )
 
 
 def lined(qkv, short_taps, medium_taps, skip_gain, w_out, resid, steer):
     channels, slab = qkv.shape[1:]
     width = resid.shape[0]
-    short = jnp.swapaxes(short_taps.astype(F32), 1, 2)
-    medium = medium_taps.astype(F32)
-    medium = jnp.concatenate([medium[:, :1] + skip_gain[:, None], medium[:, 1:]], 1).T
     whole = pl.BlockSpec(memory_space=pltpu.VMEM)
     anywhere = pl.BlockSpec(memory_space=pl.ANY)
     token = lambda: pltpu.VMEM((slab, channels), BF16)
@@ -588,7 +616,7 @@
     span = 512
     return pl.pallas_call(
         line_kernel,
-        in_specs=[anywhere] * 3 + [whole] * 3,
+        in_specs=[anywhere] * 3 + [whole] * 4,
         out_specs=[anywhere] * 4,
         out_shape=[
             jax.ShapeDtypeStruct(resid.shape, BF16),
@@ -601,6 +629,9 @@
             pltpu.VMEM((2, width // COLS, channels, COLS), BF16),
             pltpu.VMEM((2, 3, LANES, span), BF16),
             pltpu.VMEM((2, width, 256), BF16),
+            pltpu.VMEM((3, STAPS, channels), F32),
+            pltpu.VMEM((9 * PHASE, channels), F32),
+            pltpu.VMEM((LANES, channels), F32),
             pltpu.VMEM((3, span, LANES), F32),
             pltpu.VMEM((span - LANES, LANES), F32),
             pltpu.VMEM((9, EDGE + (span - LANES) // 4, LANES), F32),
@@ -608,8 +639,8 @@
             pltpu.VMEM((256, LANES), F32),
             dma((5, len(PARTS))),
             dma((5, len(PARTS))),
-            dma((2, 8)),
-            dma((2, 8)),
+            dma((2, 2, 8)),
+            dma((2, 2, 8)),
             dma,
             dma,
             dma((2, width // COLS)),
@@ -622,7 +653,7 @@
         cost_estimate=pl.CostEstimate(
             flops=12 * channels * slab * width, bytes_accessed=20 * channels * width, transcendentals=0
         ),
-    )(qkv, w_out, resid, short, nine_taps(medium), steer[None])[0]
+    )(qkv, w_out, resid, jnp.swapaxes(short_taps, 1, 2), medium_taps, skip_gain[None], steer[None])[0]
 
 
 def solution(mesh):

time: 304 us -> 269 us (0.88)
  Pallas kernels: 285 us -> 261 us
  other arithmetic: 5.45 us -> 0 us
  local copies, waits for them, and re-layouts: 9.77 us -> 4.64 us
    pallas_call x1, Pallas kernels: 285 us -> 261 us  [lined(): pl.pallas_call(line_kernel, in_specs=[anywhere] * 3 + [whole] * 4, out_sp...]
    unnamed x8 -> x1, local copies, waits for them, and re-layouts: 8.78 us -> 4.64 us
where the time goes in v2:
time: 269 us; the launch traced here: 265 us
  Pallas kernels  261 us (97%)
  local copies, waits for them, and re-layouts  4.64 us (2%)
    pallas_call x1, Pallas kernels, lined(): pl.pallas_call(line_kernel, in_specs=[anywhere] * 3 + [whole] * 4, out_sp...  261 us

profile of v2, /device:TPU:9, one launch (start us, length us, event | category | flops | bytes accessed | tf_op | source)
XLA Modules:
  0.0 265.3 jit_solution(16832636036816606605)
XLA Ops:
  0.0 260.6 %shard_map.73 = (bf16[2048,1024]{1,0:T(8,128)(2,1)}, bf16[2048,2048]{1,0:T(8,128)(2,1)}, bf16[2048,2048]{1,0:T(8,128)(2,1)}, bf16[3,2048,256]{2,1,0:T(8,128)(2,1)}) custom-call(bf16[3,2048,1024]{2,1,0:T(8,128)(2,1)} %qkv.1, bf16[2048,8192]{1,0:T(8,128)(2,1)} %w_out.1, bf16[2048,1024]{1,0:T(8,128)(2,1)} %resid.1, bf16[3,7,2048]{2,1,0:T(8,128)(2,1)} %bitcast.3, ...), custom_call_target="tpu_custom_call" | custom-call | flops 51539607552 | bytes 83886080 | tf_op jit(solution)/shard_map/pallas_call | solution.py:617
  260.6 4.6 %copy.9 = bf16[2048,1024]{1,0:T(8,128)(2,1)} copy(bf16[2048,1024]{1,0:T(8,128)(2,1)} %get-tuple-element.6) | data formatting | bytes 8388608

commit v3 on v2

--- a/solution.py
+++ b/solution.py
@@ -145,7 +145,9 @@
 COLS = 512
 VMEM_LIMIT = 62 << 20
 FEATURES = ((896, 128), (768, 128), (512, 256), (256, 256), (0, 256))
-PARTS = ((896, 128), (768, 128), (512, 256), (256, 256), (128, 128), (64, 64), (0, 64))
+PARTS = (
+    (960, 64), (896, 64), (768, 128), (640, 128), (512, 128), (384, 128), (256, 128), (128, 128), (64, 64), (0, 64),
+)
 PLANE = (2, 4, 6)
 SUM_IN, Y_IN, ACROSS_OUTER, ACROSS_INNER, SUM_OUT = range(5)
 
@@ -583,25 +585,27 @@
 
 SCHEDULE = (
     (0, 0, 11, (("plane", 0, 0),), ()),
-    (0, 11, 16, (), (("sum", 0), ("go_sum", 0))),
+    (0, 11, 16, (), (("sum", 0, 1), ("go_sum", 0, 1))),
     (1, 0, 8, (("plane", 0, 1),), ()),
-    (1, 8, 16, (), (("sum", 1), ("go_sum", 1), ("go_y", 0, 1))),
-    (2, 0, 4, (("cross", 0),), ()),
-    (2, 4, 11, (("core", 0, 0), ("cross", 1)), ()),
-    (2, 11, 16, (("core", 0, 1), ("far", 0, 1), ("far_end", 0)), (("sum", 2), ("go_sum", 2))),
-    (3, 0, 8, (("far_end", 1), ("out", 0, 1)), ()),
-    (3, 8, 16, (("cross", 2),), (("sum", 3), ("go_sum", 3))),
-    (4, 0, 14, (("cross", 3),), ()),
-    (4, 14, 16, (
-        ("near", 0, 1), ("out", 2), ("near", 2), ("plane", 1, 0), ("cross", 4), ("plane", 1, 1),
-        ("far", 2), ("far_end", 2), ("core", 1, 0), ("cross", 5), ("cross", 6), ("core", 1, 1), ("out", 3), ("near", 3),
-        ("far", 3), ("far_end", 3), ("out", 4, 5, 6), ("far", 4, 5, 6), ("far_end", 4), ("near", 4, 5, 6), ("far_end", 5), ("near_end", 0, 1), ("far_end", 6),
-        ("near_end", 2), ("near_end", 3), ("near_end", 4, 5, 6), ("final", 0, 1), ("final", 2),
-        ("final", 3), ("final", 4), ("final", 5, 6),
+    (1, 8, 15, (("cross", 0),), ()),
+    (1, 15, 16, (), (("sum", 2), ("go_sum", 2), ("go_y", 0, 1, 2))),
+    (2, 0, 2, (("cross", 1),), ()),
+    (2, 2, 11, (("core", 0, 0), ("cross", 2)), ()),
+    (2, 11, 16, (("core", 0, 1), ("far", 0, 1, 2), ("far_end", 0, 1)), (("sum", 3, 4), ("go_sum", 3, 4))),
+    (3, 0, 6, (("far_end", 2), ("cross", 3)), ()),
+    (3, 6, 11, (("cross", 4), ("out", 0, 1, 2)), ()),
+    (3, 11, 16, (), (("sum", 5, 6), ("go_sum", 5, 6))),
+    (4, 0, 4, (("cross", 5),), ()),
+    (4, 4, 12, (("cross", 6),), ()),
+    (4, 12, 16, (
+        ("far", 3, 4), ("near", 0, 1, 2), ("far_end", 3), ("out", 3, 4), ("near", 3, 4), ("far_end", 4), ("plane", 1, 0), ("far", 5, 6), ("near", 5, 6),
+        ("plane", 1, 1), ("out", 5, 6), ("cross", 7), ("core", 1, 0), ("cross", 8), ("cross", 9), ("near", 7, 8, 9), ("far_end", 5), ("out", 7, 8, 9),
+        ("far", 7, 8, 9), ("core", 1, 1), ("far_end", 6), ("near_end", 0, 1, 2), ("near_end", 3, 4), ("final", 0, 1, 2), ("far_end", 7), ("near_end", 5, 6), ("far_end", 8), ("final", 3, 4),
+        ("far_end", 9), ("near_end", 7, 8, 9), ("final", 5, 6), ("final", 7), ("final", 8, 9),
     ), (
-        ("sum", 4, 5, 6), ("go_sum", 4), ("go_w", 1), ("go_y", 2), ("go_sum", 5, 6), ("go_y", 3, 4, 5, 6),
-        ("out", 0, 1), ("out", 2), ("out", 3), ("out", 4, 5, 6),
-        ("final", 0, 1), ("final", 2), ("final", 3), ("final", 4, 5, 6),
+        ("sum", 7, 8, 9), ("go_y", 3, 4), ("go_w", 1), ("go_sum", 7, 8, 9), ("go_y", 5, 6, 7, 8, 9),
+        ("out", 0, 1, 2), ("out", 3, 4), ("out", 5, 6), ("out", 7, 8, 9),
+        ("final", 0, 1, 2), ("final", 3, 4), ("final", 5, 6), ("final", 7, 8, 9),
     )),
 )
 

time: 269 us -> 260 us (0.967)
  Pallas kernels: 261 us -> 254 us
    pallas_call x1, Pallas kernels: 261 us -> 254 us  [lined(): pl.pallas_call(line_kernel, in_specs=[anywhere] * 3 + [whole] * 4, out_sp...]
where the time goes in v3:
time: 260 us; the launch traced here: 259 us
  Pallas kernels  254 us (98%)
  local copies, waits for them, and re-layouts  4.64 us (2%)
    pallas_call x1, Pallas kernels, lined(): pl.pallas_call(line_kernel, in_specs=[anywhere] * 3 + [whole] * 4, out_sp...  254 us

profile of v3, /device:TPU:9, one launch (start us, length us, event | category | flops | bytes accessed | tf_op | source)
XLA Modules:
  0.0 258.7 jit_solution(13399374997142067184)
XLA Ops:
  0.0 254.1 %shard_map.73 = (bf16[2048,1024]{1,0:T(8,128)(2,1)}, bf16[2048,2048]{1,0:T(8,128)(2,1)}, bf16[2048,2048]{1,0:T(8,128)(2,1)}, bf16[3,2048,256]{2,1,0:T(8,128)(2,1)}) custom-call(bf16[3,2048,1024]{2,1,0:T(8,128)(2,1)} %qkv.1, bf16[2048,8192]{1,0:T(8,128)(2,1)} %w_out.1, bf16[2048,1024]{1,0:T(8,128)(2,1)} %resid.1, bf16[3,7,2048]{2,1,0:T(8,128)(2,1)} %bitcast.3, ...), custom_call_target="tpu_custom_call" | custom-call | flops 51539607552 | bytes 83886080 | tf_op jit(solution)/shard_map/pallas_call | solution.py:621
  254.1 4.6 %copy.9 = bf16[2048,1024]{1,0:T(8,128)(2,1)} copy(bf16[2048,1024]{1,0:T(8,128)(2,1)} %get-tuple-element.6) | data formatting | bytes 8388608

commit v4 on v3

--- a/solution.py
+++ b/solution.py
@@ -322,10 +322,15 @@
     class Plan:
         def __init__(self, units):
             self.units, self.at, self.ended = units, 0, set()
+            self.turn, self.runs = [], []
+            for which in units:
+                if not self.runs or self.runs[-1] != which:
+                    self.runs.append(which)
+                self.turn.append(len(self.runs) - 1)
 
         def load(self, i):
-            if i < len(self.units):
-                which = self.units[i]
+            if i < len(self.runs):
+                which = self.runs[i]
                 if which in (0, 1) and which not in self.ended:
                     self.ended.add(which)
                     relay_end(which)
@@ -333,15 +338,18 @@
                     fetch(which, i % 2, j).start()
 
         def run(self, src, parts, each):
-            i = self.at
+            turn = self.turn[self.at]
+            new = self.at == 0 or self.turn[self.at - 1] != turn
             self.at += 1
-            self.load(i + 1)
+            if new:
+                self.load(turn + 1)
             first = PARTS[parts[-1]][0]
             tokens = sum(PARTS[k][1] for k in parts)
 
             def body(j, carry):
-                fetch(self.units[i], i % 2, j).wait()
-                total = jnp.dot(src[first : first + tokens], wbuf[i % 2, j], preferred_element_type=F32)
+                if new:
+                    fetch(self.runs[turn], turn % 2, j).wait()
+                total = jnp.dot(src[first : first + tokens], wbuf[turn % 2, j], preferred_element_type=F32)
                 each(total, j, pl.ds(first, tokens), pl.ds(pl.multiple_of(j * COLS, COLS), COLS))
                 return carry
 

time: 260 us -> 259 us (level)
  no operation moved by 1% of the time
where the time goes in v4:
time: 259 us
  Pallas kernels  254 us (98%)
  local copies, waits for them, and re-layouts  4.64 us (2%)
    pallas_call x1, Pallas kernels, lined(): pl.pallas_call(line_kernel, in_specs=[anywhere] * 3 + [whole] * 4, out_sp...  254 us

profile of v4, /device:TPU:9, one launch (start us, length us, event | category | flops | bytes accessed | tf_op | source)
XLA Modules:
  0.0 258.7 jit_solution(3452304050012343023)
XLA Ops:
  0.0 254.1 %shard_map.73 = (bf16[2048,1024]{1,0:T(8,128)(2,1)}, bf16[2048,2048]{1,0:T(8,128)(2,1)}, bf16[2048,2048]{1,0:T(8,128)(2,1)}, bf16[3,2048,256]{2,1,0:T(8,128)(2,1)}) custom-call(bf16[3,2048,1024]{2,1,0:T(8,128)(2,1)} %qkv.1, bf16[2048,8192]{1,0:T(8,128)(2,1)} %w_out.1, bf16[2048,1024]{1,0:T(8,128)(2,1)} %resid.1, bf16[3,7,2048]{2,1,0:T(8,128)(2,1)} %bitcast.3, ...), custom_call_target="tpu_custom_call" | custom-call | flops 51539607552 | bytes 83886080 | tf_op jit(solution)/shard_map/pallas_call | solution.py:629
  254.1 4.6 %copy.9 = bf16[2048,1024]{1,0:T(8,128)(2,1)} copy(bf16[2048,1024]{1,0:T(8,128)(2,1)} %get-tuple-element.6) | data formatting | bytes 8388608
